TPU v7x, 256 devices: a whole 4x4x8 slice. The times are simulated.
256 devices in a mesh: replica: 8 (over z_lo, x), fsdp: 32 (over y, z_hi, core).
Axes of the slice: x: 4, y: 4, z: 8 (z_hi: 4, z_lo: 2; z = z_hi * 2 + z_lo), core: 2. Of those that a mesh axis runs over, the one named last changes fastest.
Arguments:
- hidden_in: bfloat16 [8, 12288, 8192], P('replica', 'fsdp'), may hold values from -6 to 6
- value_weight: bfloat16 [8, 8192, 512], P('replica', 'fsdp'), may hold values from -0.0625 to 0.0625
- grad_out: bfloat16 [8, 12288, 512], P('replica', 'fsdp'), may hold values from -0.0546875 to 0.0546875
- local_fragment: float32 [8, 8388608], P('replica', 'fsdp'), may hold values from -6 to 6
- global_fragment: float32 [8388608], P('fsdp'), may hold values from -6 to 6
- momentum: float32 [8388608], P('fsdp'), may hold values from -3 to 3
- residual: float32 [8, 8388608], P('replica', 'fsdp'), may hold values from -3 to 3
Outputs:
- values: bfloat16 [8, 12288, 512], P('replica', 'fsdp')
- weight_grad: float32 [8, 8192, 512], P('replica', 'fsdp')
- mixed_fragment: float32 [8, 8388608], P('replica', 'fsdp')
- new_momentum: float32 [8388608], P('fsdp')
All inputs are finite; a program needn't handle non-finite values.
Results may differ from a plain program's by a relative error of at most 0.015.
Values may be sent and summed in bfloat16 or wider, within the bound.
No kernel may reach another device: no remote copies, remote signals or barrier semaphores. Data moves between devices by JAX's collectives and lax.ppermute only.
A program may use at most 128 MiB of HBM per device.

v0:
```python
import jax
import jax.numpy as jnp
from jax import lax
from jax.sharding import PartitionSpec as P

BLOCK = 128
outer_rate = 0.7
outer_momentum = 0.9
mix_weight = 0.5


def per_device(
    hidden_in, value_weight, grad_out, local_fragment, global_fragment, momentum, residual
):
    tokens = hidden_in[0]
    weight = value_weight[0]
    cotangent = grad_out[0]
    columns = tokens
    projected = jnp.dot(
        columns,
        lax.all_gather(weight, "fsdp", axis=0, tiled=True),
        preferred_element_type=jnp.float32,
    )
    values = projected.astype(jnp.bfloat16)[None]
    local_row = local_fragment[0]
    nudged = global_fragment - local_row + residual[0]
    blocks = nudged.reshape(-1, BLOCK)
    block_scale = lax.optimization_barrier(
        (jnp.max(jnp.abs(blocks), axis=1) + 1e-06).astype(jnp.bfloat16)
    )
    block_codes = lax.optimization_barrier(
        (blocks / block_scale.astype(jnp.float32)[:, None]).astype(jnp.bfloat16)
    )
    replicas = lax.axis_size("replica")
    decoded = block_codes.astype(jnp.float32) * block_scale.astype(jnp.float32)[:, None]
    summed_all = lax.psum(decoded.astype(jnp.bfloat16), "replica").astype(jnp.float32)
    average = (summed_all / replicas).reshape(-1)
    new_momentum = outer_momentum * momentum + average
    new_global = global_fragment - outer_rate * (average + outer_momentum * new_momentum)
    mixed_fragment = mix_weight * local_row + (1.0 - mix_weight) * new_global
    columns = tokens
    grad_rows = lax.psum_scatter(
        lax.dot_general(
            columns, cotangent, (((0,), (0,)), ((), ())), preferred_element_type=jnp.float32
        ),
        "fsdp",
        scatter_dimension=0,
        tiled=True,
    )
    return (values, grad_rows[None], mixed_fragment[None], new_momentum)


def solution(mesh):
    return jax.shard_map(
        per_device,
        mesh=mesh,
        in_specs=(
            P("replica", "fsdp", None),
            P("replica", "fsdp", None),
            P("replica", "fsdp", None),
            P("replica", "fsdp"),
            P("fsdp"),
            P("fsdp"),
            P("replica", "fsdp"),
        ),
        out_specs=(
            P("replica", "fsdp", None),
            P("replica", "fsdp", None),
            P("replica", "fsdp"),
            P("fsdp"),
        ),
        check_vma=False,
    )
```

profile of v0, /device:TPU:1, one launch (start us, length us, event | category | flops | bytes accessed | tf_op | source)
XLA Modules:
  0.0 277.5 jit_solution(1331536064113307561)
XLA Ops:
  8.0 0.0 copy-start
  8.0 0.0 all-reduce.2.cloned.1.call-start
  8.1 2.2 fusion.19
  10.3 2.2 fusion.20
  12.5 1.1 multiply_convert_fusion
  13.7 0.0 all-reduce.2.cloned.1.call-update
  13.7 0.0 all-gather.3.cloned.1.call-start
  13.8 0.5 all-gather.3.cloned.1.call-update
  14.3 0.0 reduce-scatter.2.cloned.1.call-start
  14.3 0.0 copy-done
  14.3 11.1 %fusion.2 = f32[8192,512]{1,0:T(8,128)} fusion(bf16[1,384,8192]{2,1,0:T(8,128)(2,1)} %param.7, bf16[1,384,512]{2,1,0:T(8,128)(2,1)S(1)} %copy-done), kind=kOutput, calls=%fused_computation.2 | convolution fusion | flops 3221225472 | bytes 23461888 | tf_op jit(solution)/shard_map/dot_general | solution.py:43
  25.4 0.0 copy-start.1
  25.4 0.0 copy-start.2
  25.4 0.0 copy-start.3
  25.4 0.0 reduce-scatter.2.cloned.1.call-update
  25.5 85.4 %all-reduce.2.cloned.1.call-done = bf16[2048,128]{1,0:T(8,128)(2,1)} async-done(((bf16[2048,128]{1,0:T(8,128)(2,1)}), bf16[2048,128]{1,0:T(8,128)(2,1)}) %all-reduce.2.cloned.1.call-update) | async-done | bytes 524304 | tf_op jit(solution)/shard_map/psum | solution.py:36
  110.8 0.0 copy-done.1
  110.8 0.0 copy-done.2
  110.8 0.0 copy-done.3
  110.8 2.7 fusion.18
  113.5 0.0 all-gather.3.cloned.1.call-done
  113.5 10.4 %fusion.10 = bf16[1,384,512]{2,1,0:T(8,128)(2,1)} fusion(bf16[1,8192,512]{2,1,0:T(8,128)(2,1)} %all-gather.3.cloned.1.call-done, bf16[1,384,8192]{2,1,0:T(8,128)(2,1)} %param.7), kind=kOutput, calls=%fused_computation.6 | convolution fusion | flops 3221422080 | bytes 15073280 | tf_op jit(solution)/shard_map/dot_general | solution.py:19
  124.0 146.1 %reduce-scatter.2.cloned.1.call-done = f32[256,512]{1,0:T(8,128)} async-done(((f32[8192,512]{1,0:T(8,128)}), f32[256,512]{1,0:T(8,128)}) %reduce-scatter.2.cloned.1.call-update) | async-done | bytes 524304 | tf_op jit(solution)/shard_map/reduce_scatter | solution.py:42
  (2 shorter events, 0.0 us)
Async XLA Ops:
  8.0 6.3 %copy-start = (bf16[1,384,512]{2,1,0:T(8,128)(2,1)S(1)}, bf16[1,384,512]{2,1,0:T(8,128)(2,1)}, u32[]{:S(2)}) copy-start(bf16[1,384,512]{2,1,0:T(8,128)(2,1)} %param.9) | copy-start | bytes 1179652
  8.0 102.8 %all-reduce.2.cloned.1.call-start = ((), (), s32[]{:S(2)}) async-start(), calls=%async_computation.2 | async-start | bytes 1048576 | tf_op jit(solution)/shard_map/psum | solution.py:36
  13.7 99.8 %all-gather.3.cloned.1.call-start = ((), (), s32[]{:S(2)}) async-start(), calls=%async_computation.3 | async-start | bytes 8650752 | tf_op jit(solution)/shard_map/all_gather | solution.py:21
  14.3 255.7 %reduce-scatter.2.cloned.1.call-start = ((), (), s32[]{:S(2)}) async-start(), calls=%async_computation.1 | async-start | bytes 17301504 | tf_op jit(solution)/shard_map/reduce_scatter | solution.py:42
  25.4 85.4 %copy-start.1 = (f32[1,262144]{1,0:T(1,128)S(1)}, f32[1,262144]{1,0:T(1,128)}, u32[]{:S(2)}) copy-start(f32[1,262144]{1,0:T(1,128)} %param.10) | copy-start | bytes 3145732
  25.4 85.4 %copy-start.2 = (f32[262144]{0:T(1024)S(1)}, f32[262144]{0:T(1024)}, u32[]{:S(2)}) copy-start(f32[262144]{0:T(1024)} %param.11) | copy-start | bytes 3145732
  25.4 85.4 %copy-start.3 = (f32[262144]{0:T(1024)S(1)}, f32[262144]{0:T(1024)}, u32[]{:S(2)}) copy-start(f32[262144]{0:T(1024)} %param.12) | copy-start | bytes 3145732
Sparse Core Ops, SparseCore 0:
  13.8 96.9 all-reduce.1
Sparse Core Ops, SparseCore 1:
  16.7 85.2 all-gather.2
  106.6 163.3 reduce-scatter.1
where the time goes:
time: 278 us; the launch traced here: 277 us
  waiting for transfers between devices  232 us (83%)
  matrix products  21.5 us (8%)
  between operations  15.5 us (6%)
  other arithmetic  8.29 us (3%)
    reduce_scatter x1, waiting for transfers between devices, per_device(): lax.psum_scatter(lax.dot_general(columns, cotangent, (((0,), (0,)), ((),...  146 us
    psum x1, waiting for transfers between devices, per_device(): lax.psum(decoded.astype(jnp.bfloat16), 'replica').astype(jnp.float32)  85.4 us
    dot_general x1, matrix products, per_device(): lax.dot_general(columns, cotangent, (((0,), (0,)), ((), ())), preferred_e...  11.1 us
    dot_general x1, matrix products, per_device(): jnp.dot(columns, lax.all_gather(weight, 'fsdp', axis=0, tiled=True), pref...  10.4 us
  transfers between devices with their start and end apart: 3, of which 2 were waited for; matrix products, arithmetic and copies ran while one was open for 9% of the time, Pallas kernels for 0%

commit v1 on v0

--- a/solution.py
+++ b/solution.py
@@ -33,7 +33,9 @@
     )
     replicas = lax.axis_size("replica")
     decoded = block_codes.astype(jnp.float32) * block_scale.astype(jnp.float32)[:, None]
-    summed_all = lax.psum(decoded.astype(jnp.bfloat16), "replica").astype(jnp.float32)
+    summed_all = jnp.sum(lax.all_gather(decoded.astype(jnp.bfloat16), "replica"), axis=0).astype(
+        jnp.float32
+    )
     average = (summed_all / replicas).reshape(-1)
     new_momentum = outer_momentum * momentum + average
     new_global = global_fragment - outer_rate * (average + outer_momentum * new_momentum)

time: 278 us -> 328 us (1.18)
  waiting for transfers between devices: 232 us -> 282 us
    psum x1 -> x0, waiting for transfers between devices: 85.4 us -> none  [per_device(): lax.psum(decoded.astype(jnp.bfloat16), 'replica').astype(jnp.float32)]
    all_gather x1, waiting for transfers between devices: 0.01 us -> 71.9 us  [per_device(): lax.all_gather(weight, 'fsdp', axis=0, tiled=True)]
    all_gather x0 -> x1, waiting for transfers between devices: none -> 47.2 us  [per_device(): lax.all_gather(decoded.astype(jnp.bfloat16), 'replica')]
    reduce_scatter x1, waiting for transfers between devices: 146 us -> 162 us  [per_device(): lax.psum_scatter(lax.dot_general(columns, cotangent, (((0,), (0,)), ((),...]
  transfers between devices with their start and end apart: 3 -> 3, of which waited for: 2 -> 3; matrix products, arithmetic and copies ran while one was open for 9% -> 8% of each run, Pallas kernels for 0% -> 0%
where the time goes in v1:
time: 328 us
  waiting for transfers between devices  282 us (86%)
  matrix products  20.4 us (6%)
  between operations  13.8 us (4%)
  other arithmetic  11.5 us (4%)
    reduce_scatter x1, waiting for transfers between devices, per_device(): lax.psum_scatter(lax.dot_general(columns, cotangent, (((0,), (0,)), ((),...  162 us
    all_gather x1, waiting for transfers between devices, per_device(): lax.all_gather(weight, 'fsdp', axis=0, tiled=True)  71.9 us
    all_gather x1, waiting for transfers between devices, per_device(): lax.all_gather(decoded.astype(jnp.bfloat16), 'replica')  47.2 us
    dot_general x1, matrix products, per_device(): lax.dot_general(columns, cotangent, (((0,), (0,)), ((), ())), preferred_e...  11.1 us
    dot_general x1, matrix products, per_device(): jnp.dot(columns, lax.all_gather(weight, 'fsdp', axis=0, tiled=True), pref...  9.35 us
  transfers between devices with their start and end apart: 3, of which 3 were waited for; matrix products, arithmetic and copies ran while one was open for 8% of the time, Pallas kernels for 0%

profile of v1, /device:TPU:1, one launch (start us, length us, event | category | flops | bytes accessed | tf_op | source)
XLA Modules:
  0.0 327.9 jit_solution(298029622539860113)
XLA Ops:
  7.2 0.0 copy-start
  7.2 0.0 all-gather.7.cloned.1.call-start
  7.2 2.2 fusion.19
  9.5 2.2 fusion.20
  11.7 1.1 multiply_convert_fusion
  12.8 0.0 all-gather.7.cloned.1.call-update
  12.9 0.0 all-gather.5.cloned.1.call-start
  12.9 0.7 all-gather.5.cloned.1.call-update
  13.6 0.0 reduce-scatter.2.cloned.1.call-start
  13.7 0.0 copy-done
  13.7 11.1 %fusion.2 = f32[8192,512]{1,0:T(8,128)} fusion(bf16[1,384,8192]{2,1,0:T(8,128)(2,1)} %param.7, bf16[1,384,512]{2,1,0:T(8,128)(2,1)S(1)} %copy-done), kind=kOutput, calls=%fused_computation.2 | convolution fusion | flops 3221225472 | bytes 23461888 | tf_op jit(solution)/shard_map/dot_general | solution.py:45
  24.8 0.0 copy-start.1
  24.8 0.0 copy-start.2
  24.8 0.0 reduce-scatter.2.cloned.1.call-update
  24.8 47.2 %all-gather.7.cloned.1.call-done = bf16[16384,128]{1,0:T(8,128)(2,1)} async-done(((bf16[2048,128]{1,0:T(8,128)(2,1)}), bf16[16384,128]{1,0:T(8,128)(2,1)}) %all-gather.7.cloned.1.call-update) | async-done | bytes 4194320 | tf_op jit(solution)/shard_map/all_gather | solution.py:36
  72.0 3.1 reduce_sum.12
  75.1 0.0 copy-done.1
  75.1 0.0 copy-done.2
  75.1 2.9 fusion.18
  78.0 71.9 %all-gather.5.cloned.1.call-done = bf16[1,8192,512]{2,1,0:T(8,128)(2,1)} async-done(((bf16[1,256,512]{2,1,0:T(8,128)(2,1)}), bf16[1,8192,512]{2,1,0:T(8,128)(2,1)}) %all-gather.5.cloned.1.call-update) | async-done | bytes 8388624 | tf_op jit(solution)/shard_map/all_gather | solution.py:21
  149.9 9.3 %fusion.10 = bf16[1,384,512]{2,1,0:T(8,128)(2,1)} fusion(bf16[1,8192,512]{2,1,0:T(8,128)(2,1)} %all-gather.5.cloned.1.call-done, bf16[1,384,8192]{2,1,0:T(8,128)(2,1)} %param.7), kind=kOutput, calls=%fused_computation.6 | convolution fusion | flops 3221422080 | bytes 15073280 | tf_op jit(solution)/shard_map/dot_general | solution.py:19
  159.2 162.2 %reduce-scatter.2.cloned.1.call-done = f32[256,512]{1,0:T(8,128)} async-done(((f32[8192,512]{1,0:T(8,128)}), f32[256,512]{1,0:T(8,128)}) %reduce-scatter.2.cloned.1.call-update) | async-done | bytes 524304 | tf_op jit(solution)/shard_map/reduce_scatter | solution.py:44
  (2 shorter events, 0.0 us)
Async XLA Ops:
  7.2 6.5 %copy-start = (bf16[1,384,512]{2,1,0:T(8,128)(2,1)S(1)}, bf16[1,384,512]{2,1,0:T(8,128)(2,1)}, u32[]{:S(2)}) copy-start(bf16[1,384,512]{2,1,0:T(8,128)(2,1)} %param.9) | copy-start | bytes 1179652
  7.2 64.8 %all-gather.7.cloned.1.call-start = ((), (), s32[]{:S(2)}) async-start(), calls=%async_computation.3 | async-start | bytes 4718592 | tf_op jit(solution)/shard_map/all_gather | solution.py:36
  12.9 137.0 %all-gather.5.cloned.1.call-start = ((), (), s32[]{:S(2)}) async-start(), calls=%async_computation.2 | async-start | bytes 8650752 | tf_op jit(solution)/shard_map/all_gather | solution.py:21
  13.6 307.8 %reduce-scatter.2.cloned.1.call-start = ((), (), s32[]{:S(2)}) async-start(), calls=%async_computation.1 | async-start | bytes 17301504 | tf_op jit(solution)/shard_map/reduce_scatter | solution.py:44
  24.8 50.3 %copy-start.1 = (f32[262144]{0:T(1024)S(1)}, f32[262144]{0:T(1024)}, u32[]{:S(2)}) copy-start(f32[262144]{0:T(1024)} %param.11) | copy-start | bytes 3145732
  24.8 50.3 %copy-start.2 = (f32[1,262144]{1,0:T(1,128)S(1)}, f32[1,262144]{1,0:T(1,128)}, u32[]{:S(2)}) copy-start(f32[1,262144]{1,0:T(1,128)} %param.10) | copy-start | bytes 3145732
Sparse Core Ops, SparseCore 0:
  13.0 58.9 all-gather.6
  74.6 75.2 all-gather.4
  154.7 166.7 reduce-scatter.1
